TPU v7x, 512 devices: a whole 4x8x8 slice. The times are simulated.
512 devices in a mesh: blk: 64 (over z_lo, x, y), grp: 8 (over z_hi, core).
Axes of the slice: x: 4, y: 8, z: 8 (z_hi: 4, z_lo: 2; z = z_hi * 2 + z_lo), core: 2. Of those that a mesh axis runs over, the one named last changes fastest.
Arguments:
- queries: bfloat16 [4096, 32, 128], P(('blk', 'grp')), may hold values from -6 to 6
- query_lens: int32 [4096], P(('blk', 'grp')), may hold values from 8 to 32
- documents: bfloat16 [512, 256, 128], P(('blk', 'grp')), may hold values from -6 to 6
- doc_lens: int32 [512], P(('blk', 'grp')), may hold values from 32 to 256
- positives: int32 [4096], P(('blk', 'grp')), may hold values from 0 to 63
Outputs:
- score_grad: float32 [4096, 3, 128], P(('blk', 'grp'))
- query_losses: float32 [4096, 3], P(('blk', 'grp'))
All inputs are finite; a program needn't handle non-finite values.
Results may differ from a plain program's by a relative error of at most 0.00095.
Values may be sent and summed in bfloat16 or wider, within the bound.
A program may use at most 64 MiB of HBM per device.

v0:
```python
import math

import jax
import jax.numpy as jnp
from jax import lax
from jax.sharding import PartitionSpec as P

inverse_heat = 0.05
far_below = 1e30
epsilon = 1e-06
prefixes = (64, 96, 128)


def shifted(shard, axis, by):
    size = lax.axis_size(axis)
    pairs = [(i, i + by) for i in range(size) if 0 <= i + by < size]
    return lax.ppermute(shard, axis, pairs)


def prefix_norms(tokens):
    values = tokens.astype(jnp.float32)
    squares = values * values
    first = jnp.sum(squares[..., :64], axis=-1)
    second = first + jnp.sum(squares[..., 64:96], axis=-1)
    third = second + jnp.sum(squares[..., 96:], axis=-1)
    return lax.rsqrt(jnp.stack([first, second, third], axis=-1) + epsilon)


def contrast(unnormalized_energies, positives, valid):
    held = jnp.where(valid, unnormalized_energies, -far_below)
    highest = jnp.max(held, axis=-1, keepdims=True)
    weights = jnp.where(valid, jnp.exp(held - highest), 0.0)
    totals = jnp.sum(weights, axis=-1, keepdims=True)
    columns = lax.broadcasted_iota(jnp.int32, unnormalized_energies.shape, 2)
    target = unnormalized_energies.shape[2] // 2 + positives
    chosen = (columns == target[:, None, None]).astype(jnp.float32)
    picked = jnp.sum(unnormalized_energies * chosen, axis=-1)
    losses = jnp.log(totals[..., 0]) + highest[..., 0] - picked
    return (weights / totals - chosen, losses)


def block_scores(query_tok, question_alive_bits, doc_tok, doc_live):
    lane_ordinal, question_span_size, width = query_tok.shape
    passage_tally, doc_len = doc_live.shape
    rows = query_tok.reshape(lane_ordinal * question_span_size, width)
    columns = doc_tok.reshape(passage_tally * doc_len, width)
    row_vector_norms = prefix_norms(rows)
    column_norms = prefix_norms(columns)
    open_slots = doc_live.reshape(passage_tally * doc_len) > 0.5
    contract_last = (((1,), (1,)), ((), ()))
    partial_dots = tuple(
        (
            lax.dot_general(
                rows[:, :prefix],
                columns[:, :prefix],
                contract_last,
                preferred_element_type=jnp.float32,
            )
            for prefix in prefixes
        )
    )
    live_rows = question_alive_bits.astype(jnp.float32)
    nested_dimension_weights = []
    for position in range(3):
        cosine = partial_dots[position] * column_norms[:, position][None, :]
        cosine = jnp.where(open_slots[None, :], cosine, -far_below)
        peak_affinity = (
            jnp.max(
                cosine.reshape(lane_ordinal * question_span_size, passage_tally, doc_len), axis=2
            )
            * row_vector_norms[:, position][:, None]
        )
        nested_dimension_weights.append(
            jnp.sum(
                peak_affinity.reshape(lane_ordinal, question_span_size, passage_tally)
                * live_rows[:, :, None],
                axis=1,
            )
            / inverse_heat
        )
    return jnp.stack(nested_dimension_weights, axis=1)


def doc_folder(query_tok, question_alive_bits, carry, piece, start):
    doc_tok, doc_live = piece
    passage_tally = doc_tok.shape[0]
    step_size = math.gcd(passage_tally, 4)
    stacked = (
        doc_tok.reshape(passage_tally // step_size, step_size, doc_tok.shape[1], doc_tok.shape[2]),
        doc_live.reshape(passage_tally // step_size, step_size, doc_live.shape[1]),
    )
    blocks = lax.map(
        lambda block_pair: block_scores(
            query_tok, question_alive_bits, block_pair[0], block_pair[1]
        ),
        stacked,
    )
    scores = jnp.transpose(blocks, (1, 2, 0, 3)).reshape(query_tok.shape[0], 3, passage_tally)
    return lax.dynamic_update_slice_in_dim(carry, scores, start, 2)


def cycle_scores(query_tok, question_alive_bits, documents, doc_live):
    empty = jnp.zeros(
        (query_tok.shape[0], 3, documents.shape[0] * lax.axis_size("blk")), jnp.float32
    )
    return doc_folder(
        query_tok,
        question_alive_bits,
        empty,
        (
            lax.all_gather(documents, "blk", axis=0, tiled=True),
            lax.all_gather(doc_live, "blk", axis=0, tiled=True),
        ),
        jnp.int32(0),
    )


def prior_documents(documents, doc_live):
    return shifted((documents, doc_live), "grp", 1)


def on_device(queries, query_lens, documents, doc_lens, positives):
    query_count, question_span_size, width = queries.shape
    passage_tally, doc_len, width_again = documents.shape
    question_alive_bits = (
        lax.broadcasted_iota(jnp.int32, (query_count, question_span_size), 1) < query_lens[:, None]
    ).astype(jnp.bfloat16)
    doc_live = (
        lax.broadcasted_iota(jnp.int32, (passage_tally, doc_len), 1) < doc_lens[:, None]
    ).astype(jnp.bfloat16)
    blocks_count = lax.axis_size("blk")
    group_docs = passage_tally * blocks_count
    own = cycle_scores(queries, question_alive_bits, documents, doc_live)
    prior_docs, prior_live = prior_documents(documents, doc_live)
    empty = jnp.zeros((query_count, 3, group_docs), jnp.float32)
    prior = doc_folder(
        queries,
        question_alive_bits,
        empty,
        (
            lax.all_gather(prior_docs, "blk", axis=0, tiled=True),
            lax.all_gather(prior_live, "blk", axis=0, tiled=True),
        ),
        jnp.int32(0),
    )
    unnormalized_energies = jnp.concatenate([prior, own], axis=2)
    columns = lax.broadcasted_iota(jnp.int32, unnormalized_energies.shape, 2)
    valid = jnp.logical_or(columns >= group_docs, lax.axis_index("grp") > 0)
    score_grad, query_losses = contrast(unnormalized_energies, positives, valid)
    return (score_grad, query_losses)


def solution(mesh):
    in_specs = (
        P(("blk", "grp"), None, None),
        P(("blk", "grp")),
        P(("blk", "grp"), None, None),
        P(("blk", "grp")),
        P(("blk", "grp")),
    )
    out_specs = (P(("blk", "grp"), None, None), P(("blk", "grp"), None))
    return jax.shard_map(
        on_device, mesh=mesh, in_specs=in_specs, out_specs=out_specs, check_vma=False
    )
```

profile of v0, /device:TPU:8, one launch (start us, length us, event | category | flops | bytes accessed | tf_op | source)
XLA Modules:
  0.0 718.8 jit_solution(13083164130419045417)
XLA Ops:
  7.9 1.7 collective-permute-start.1
  10.4 6.4 collective-permute-start
  17.4 153.0 %all-gather.1 = bf16[64,1,256]{2,1,0:T(2,128)(2,1)S(1)} all-gather(bf16[1,1,256]{2,1,0:T(2,128)(2,1)S(1)} %fusion.29), channel_id=1, replica_groups=mesh['blk'=64,'grp'=8] {'blk'}, dimensions={0}, use_global_device_ids=true | all-gather | bytes 33280 | tf_op jit(solution)/shard_map/all_gather | solution.py:112
  170.6 154.9 %all-gather = bf16[64,1,256]{2,1,0:T(2,128)(2,1)S(1)} all-gather(bf16[1,1,256]{2,1,0:T(2,128)(2,1)S(1)} %bitcast.214), channel_id=1, replica_groups=mesh['blk'=64,'grp'=8] {'blk'}, dimensions={0}, use_global_device_ids=true | all-gather | bytes 33280 | tf_op jit(solution)/shard_map/all_gather | solution.py:142
  326.4 82.6 %while.23 = (s32[]{:T(128)}, f32[16,8,3,4]{1,3,2,0:T(4,128)S(1)}, bf16[16,4,256]{2,1,0:T(4,128)(2,1)S(1)}, bf16[16,4,256,128]{3,2,1,0:T(8,128)(2,1)}, bf16[8,32,128]{2,1,0:T(8,128)(2,1)}, /*index=5*/s32[8]{0:T(128)}, s32[]{:T(128)}) while((s32[]{:T(128)}, f32[16,8,3,4]{1,3,2,0:T(4,128)S(1)}, bf16[16,4,256]{2,1,0:T(4,128)(2,1)S(1)}, ...), condition=%wide.region_27.28_spmd.clone, body=%wide.region_14.27_spmd.clone.sunk | while | flops 153864128 | bytes 3604913 | solution.py:92
  333.6 1.2 bitcast_reduce_fusion.17
  338.8 1.2 bitcast_reduce_fusion.17
  343.9 1.2 bitcast_reduce_fusion.17
  349.1 1.2 bitcast_reduce_fusion.17
  354.3 1.2 bitcast_reduce_fusion.17
  359.4 1.2 bitcast_reduce_fusion.17
  369.8 1.2 bitcast_reduce_fusion.17
  380.1 1.2 bitcast_reduce_fusion.17
  385.3 1.2 bitcast_reduce_fusion.17
  390.4 1.2 bitcast_reduce_fusion.17
  409.2 218.3 %all-gather.5.cloned.1.call-done = bf16[64,256,128]{2,1,0:T(8,128)(2,1)} async-done(((bf16[1,256,128]{2,1,0:T(8,128)(2,1)}), bf16[64,256,128]{2,1,0:T(8,128)(2,1)}) %all-gather.5.cloned.1.call-update) | async-done | bytes 4194320 | tf_op jit(solution)/shard_map/all_gather | solution.py:141
  627.5 82.7 %while.22 = (s32[]{:T(128)}, f32[16,8,3,4]{1,3,2,0:T(4,128)S(1)}, bf16[16,4,256]{2,1,0:T(4,128)(2,1)S(1)}, bf16[16,4,256,128]{3,2,1,0:T(8,128)(2,1)}, bf16[8,32,128]{2,1,0:T(8,128)(2,1)}, /*index=5*/s32[8]{0:T(128)}, s32[]{:T(128)}) while((s32[]{:T(128)}, f32[16,8,3,4]{1,3,2,0:T(4,128)S(1)}, bf16[16,4,256]{2,1,0:T(4,128)(2,1)S(1)}, ...), condition=%wide.region_13.14_spmd.clone, body=%wide.region_0.13_spmd.clone.sunk | while | flops 153864128 | bytes 3604913 | solution.py:92
  634.7 1.2 bitcast_reduce_fusion.14
  639.9 1.2 bitcast_reduce_fusion.14
  645.1 1.2 bitcast_reduce_fusion.14
  650.2 1.2 bitcast_reduce_fusion.14
  655.4 1.2 bitcast_reduce_fusion.14
  660.6 1.2 bitcast_reduce_fusion.14
  665.7 1.2 bitcast_reduce_fusion.14
  670.9 1.2 bitcast_reduce_fusion.14
  676.1 1.2 bitcast_reduce_fusion.14
  681.2 1.2 bitcast_reduce_fusion.14
  686.4 1.2 bitcast_reduce_fusion.14
  691.6 1.2 bitcast_reduce_fusion.14
  696.8 1.2 bitcast_reduce_fusion.14
  701.9 1.2 bitcast_reduce_fusion.14
  707.1 1.2 bitcast_reduce_fusion.14
  (1058 shorter events, 134.5 us)
Async XLA Ops:
  7.2 319.2 %all-gather.7.cloned.1.call-start = ((), (), s32[]{:S(2)}) async-start(), calls=%async_computation.1 | async-start | bytes 4259840 | tf_op jit(solution)/shard_map/all_gather | solution.py:111
  7.9 619.6 %all-gather.5.cloned.1.call-start = ((), (), s32[]{:S(2)}) async-start(), calls=%async_computation | async-start | bytes 4259840 | tf_op jit(solution)/shard_map/all_gather | solution.py:141
  7.9 317.7 %collective-permute-start.1 = (bf16[1,256,128]{2,1,0:T(8,128)(2,1)}, bf16[1,256,128]{2,1,0:T(8,128)(2,1)S(1)}, u32[]{:S(2)}, u32[]{:S(2)}) collective-permute-start(bf16[1,256,128]{2,1,0:T(8,128)(2,1)} %param.11), channel_id=1, source_target_pairs={{0,1},{1,2},{2,3},{3,4},{4,5},{5,6},{6,7},{8,9},{9,10},{10,11},{11... | collective-permute-start | bytes 196616 | tf_op jit(solution)/shard_map/ppermute | solution.py:17
  10.4 160.3 %collective-permute-start = (bf16[1,256]{1,0:T(2,128)(2,1)S(1)}, bf16[1,256]{1,0:T(2,128)(2,1)S(1)}, u32[]{:S(2)}, u32[]{:S(2)}) collective-permute-start(bf16[1,256]{1,0:T(2,128)(2,1)S(1)} %compare_convert_fusion), channel_id=1, source_target_pairs={{0,1},{1,2},{2,3},{3,4},{4,5},{5,6},{6,7},{8,9},{9,10},{10,11},{11... | collective-permute-start | bytes 1544 | tf_op jit(solution)/shard_map/ppermute | solution.py:17
  326.4 4.9 copy-start.3
  331.6 4.9 copy-start.3
  336.8 4.9 copy-start.3
  341.9 4.9 copy-start.3
  347.1 4.9 copy-start.3
  357.4 4.9 copy-start.3
  362.6 4.9 copy-start.3
  367.8 4.9 copy-start.3
  372.9 4.9 copy-start.3
  378.1 4.9 copy-start.3
  388.4 4.9 copy-start.3
  393.6 4.9 copy-start.3
  627.5 4.9 copy-start.4
  632.7 4.9 copy-start.4
  637.9 4.9 copy-start.4
  643.0 4.9 copy-start.4
  648.2 4.9 copy-start.4
  653.4 4.9 copy-start.4
  658.5 4.9 copy-start.4
  663.7 4.9 copy-start.4
  668.9 4.9 copy-start.4
  674.1 4.9 copy-start.4
  679.2 4.9 copy-start.4
  684.4 4.9 copy-start.4
  689.6 4.9 copy-start.4
  694.7 4.9 copy-start.4
  699.9 4.9 copy-start.4
  705.1 4.9 copy-start.4
  (37 other events, 126.8 us)
Sparse Core Ops, SparseCore 0:
  10.1 310.2 all-gather.6
  326.5 300.9 all-gather.4
where the time goes:
time: 721 us; the launch traced here: 719 us
  blocking collectives  308 us (43%)
  waiting for transfers between devices  219 us (30%)
  matrix products  63.5 us (9%)
  other arithmetic  51.2 us (7%)
  local copies, waits for them, and re-layouts  49.5 us (7%)
  between operations  14.8 us (2%)
  starting transfers between devices  8.18 us (1%)
    all_gather x1, waiting for transfers between devices, on_device(): lax.all_gather(prior_docs, 'blk', axis=0, tiled=True)  218 us
    all_gather x1, blocking collectives, on_device(): lax.all_gather(prior_live, 'blk', axis=0, tiled=True)  155 us
    all_gather x1, blocking collectives, cycle_scores(): lax.all_gather(doc_live, 'blk', axis=0, tiled=True)  153 us
    dot_general x96, matrix products, block_scores(): lax.dot_general(rows[:, :prefix], columns[:, :prefix], contract_last, pre...  63.5 us
    dynamic_slice x32, local copies, waits for them, and re-layouts, doc_folder(): lax.map(lambda block_pair: block_scores(query_tok, question_alive_bits, b...  32.1 us
    reduce_sum x64, other arithmetic, prefix_norms(): third = second + jnp.sum(squares[..., 96:], axis=-1)  28.2 us
  transfers between devices with their start and end apart: 4, of which 1 were waited for; matrix products, arithmetic and copies ran while one was open for 11% of the time, Pallas kernels for 0%

commit v1 on v0

v1 whole, which is shorter than its diff:
```python
import functools

import jax
import jax.numpy as jnp
from jax import lax
from jax.experimental import pallas as pl
from jax.experimental.pallas import tpu as pltpu
from jax.sharding import PartitionSpec as P

MESH = pl.DeviceIdType.MESH
F32 = jnp.float32
BF16 = jnp.bfloat16
EPS = 1e-06
FAR = 1e30
HEAT = 20.0
PREFIXES = (64, 96, 128)
NX, NY, NZ = 4, 8, 2
LAST = (((1,), (1,)), ((), ()))


def offset(k):
    return ((k + 1) // 2) * (2 * (k % 2) - 1)


def kernel(
    q_ref, d_ref, qlen_ref, dlen_ref, pos_ref, grad_ref, loss_ref,
    qs, ws, ds, rd, peaks, piece, parts, frame,
    q_send, q_recv, d_send, d_recv, p_send, p_recv, r_send, r_recv,
):
    blk, grp = lax.axis_index("blk"), lax.axis_index("grp")
    zl, x, y = blk // (NX * NY), (blk // NY) % NX, blk % NY
    n_grp = lax.axis_size("grp")

    def at(z_, x_, y_):
        return ((z_ * NX + x_) * NY + y_, grp)

    def along_y(by):
        return at(zl, x, (y + by + NY) % NY)

    def along_xz(a, b):
        return at((zl + a) % NZ, (x + b + NX) % NX, y)

    def remote(src, dst, send, recv, to):
        return pltpu.make_async_remote_copy(
            src_ref=src, dst_ref=dst, send_sem=send, recv_sem=recv, device_id=to, device_id_type=MESH
        )

    plane = [(a, b) for a in range(NZ) for b in range(NX) if (a, b) != (0, 0)]
    after, before = (blk, (grp + 1) % n_grp), (blk, (grp + n_grp - 1) % n_grp)

    barrier = pltpu.get_barrier_semaphore()
    senders = [along_y(by) for by in range(1, NY)] + [along_xz(a, b) for a, b in plane] + [before]
    for other in senders:
        pl.semaphore_signal(barrier, inc=1, device_id=other, device_id_type=MESH)

    tokens = lax.broadcasted_iota(jnp.int32, (32, 128), 0)
    for i in range(8):
        rows = q_ref[pl.ds(32 * i, 32), :].astype(F32)
        qs[0, pl.ds(32 * i, 32), :] = jnp.where(tokens < qlen_ref[i], rows, 0.0).astype(BF16)
    doc = d_ref[...].astype(F32)
    slots = lax.broadcasted_iota(jnp.int32, (256, 128), 0)
    ds[1, 0, 0] = jnp.where(slots < dlen_ref[0], doc, doc[0:1, :]).astype(BF16)

    pl.semaphore_wait(barrier, len(senders))

    def prior_copy():
        return remote(ds.at[1, 0, 0], ds.at[0, 0, 0], p_send.at[0], p_recv.at[0], after)

    def query_copy(k):
        return remote(qs.at[0], qs.at[k], q_send.at[k], q_recv.at[k], along_y(offset(k)))

    def doc_copy(half, a, b):
        i = half * 8 + a * 4 + b
        return remote(ds.at[half, 0, 0], ds.at[half, a, b], d_send.at[i], d_recv.at[i], along_xz(a, b))

    prior_copy().start()
    order = [(0, 1), (0, 3), (1, 0), (0, 2), (1, 1), (1, 3), (1, 2)]
    for k in (1, 2):
        query_copy(k).start()
    for a, b in order:
        doc_copy(1, a, b).start()
    for k in (3, 4, 5, 6, 7):
        query_copy(k).start()

    lanes = lax.broadcasted_iota(jnp.int32, (256, 128), 1)

    def make_weights(k):
        q = qs[k].astype(F32)
        for p in range(2):
            ws[k, p] = jnp.where(lanes < PREFIXES[p], q, 0.0).astype(BF16)
        ws[k, 2] = qs[k]

    make_weights(0)
    prior_copy().wait_recv()
    for a, b in order:
        doc_copy(0, a, b).start()

    def make_norms(half, a, b):
        values = ds[half, a, b].astype(F32)
        squares = values * values
        total = jnp.zeros((256, 1), F32)
        low = 0
        for p, high in enumerate(PREFIXES):
            part = jnp.where((lanes >= low) & (lanes < high), squares, 0.0)
            total = total + jnp.sum(part, axis=1, keepdims=True)
            rd[p, half, a, b] = jnp.broadcast_to(lax.rsqrt(total + EPS), (256, 128))
            low = high

    def job(k, half, a):
        docs = ds[half, a].reshape(1024, 128)
        for p in range(3):
            dots = lax.dot_general(docs, ws[k, p], LAST, preferred_element_type=F32)
            scale = rd[p, half, a].reshape(1024, 128)
            for c in range(2):
                scaled = dots[:, c * 128 : (c + 1) * 128] * scale
                best = jnp.max(scaled.reshape(4, 32, 8, 128), axis=1)
                peaks[k, p, half, a, :, :, pl.ds(c * 128, 128)] = best

    def wait_docs(half, a):
        for b in range(NX):
            if isinstance(a, int) and a == 0 and b == 0:
                continue
            doc_copy(half, a, b).wait_recv()

    prefix_rows = lax.broadcasted_iota(jnp.int32, (8, 128), 0)
    prefix_lanes = lax.broadcasted_iota(jnp.int32, (8, 128), 1)
    limit = jnp.where(prefix_rows == 0, 64, jnp.where(prefix_rows == 1, 96, 128))
    below = (prefix_lanes < limit).astype(F32).astype(BF16)
    seg_rows = lax.broadcasted_iota(jnp.int32, (128, 256), 0)
    seg_query = lax.broadcasted_iota(jnp.int32, (128, 256), 1) // 32

    def split(value):
        high = value.astype(BF16)
        return high, value - high.astype(F32)

    def finish(k):
        q = qs[k].astype(F32)
        high, rest = split(q * q)
        sums = lax.dot_general(below, high, LAST, preferred_element_type=F32)
        sums += lax.dot_general(below, rest.astype(BF16), LAST, preferred_element_type=F32)
        rq = lax.rsqrt(sums + EPS) * HEAT
        total = jnp.zeros((16, 128), F32)
        for p in range(3):
            best = jnp.max(peaks[k, p].reshape(16, 8, 256), axis=1) * rq[p : p + 1, :]
            seg = (seg_rows == seg_query + 8 * p).astype(F32).astype(BF16)
            high, rest = split(best)
            middle, rest = split(rest)
            for part in (high, middle, rest.astype(BF16)):
                total += lax.dot_general(part, seg, LAST, preferred_element_type=F32)
        return total

    def back_copy(k):
        return remote(piece.at[k], parts.at[y], r_send.at[k], r_recv.at[k], along_y(-offset(k)))

    for k in (1, 2):
        query_copy(k).wait_recv()
        make_weights(k)
    for half in (1, 0):
        for a in range(NZ):
            wait_docs(half, a)

            def norms(b, carry):
                make_norms(half, a, b)
                return carry

            lax.fori_loop(0, NX, norms, 0)

            def near(k, carry):
                job(k, half, a)
                return carry

            lax.fori_loop(1, 3, near, 0)

    def send_back(k, carry):
        piece[k] = finish(k)
        back_copy(k).start()
        return carry

    lax.fori_loop(1, 3, send_back, 0)

    def far(k, carry):
        query_copy(k).wait_recv()
        make_weights(k)

        def one(i, inner):
            job(k, i // 2, i % 2)
            return inner

        lax.fori_loop(0, 4, one, 0)
        return send_back(k, carry)

    lax.fori_loop(3, 8, far, 0)

    def own(i, carry):
        job(0, i // 2, i % 2)
        return carry

    lax.fori_loop(0, 4, own, 0)
    parts[y] = finish(0)

    for k in range(1, NY):
        back_copy(k).wait_recv()

    for half in range(2):
        for a in range(NZ):
            for b in range(NX):
                row = half * 8 + a * 4 + b
                column = half * 8 + ((zl + a) % NZ) * 4 + (x - b + NX) % NX
                frame[column] = parts[:, row, :]
    logits = jnp.transpose(frame[...].reshape(128, 128))
    columns = lax.broadcasted_iota(jnp.int32, (8, 128), 1)
    rows = lax.broadcasted_iota(jnp.int32, (8, 128), 0)
    valid = jnp.logical_or(columns >= 64, grp > 0)
    target = jnp.zeros((8, 128), jnp.int32)
    for i in range(8):
        target = jnp.where(rows == i, pos_ref[i] + 64, target)
    chosen = (columns == target).astype(F32)
    for p in range(3):
        value = logits[8 * p : 8 * p + 8, :]
        held = jnp.where(valid, value, -FAR)
        highest = jnp.max(held, axis=1, keepdims=True)
        weights = jnp.where(valid, jnp.exp(held - highest), 0.0)
        total = jnp.sum(weights, axis=1, keepdims=True)
        picked = jnp.sum(jnp.where(columns == target, value, 0.0), axis=1, keepdims=True)
        grad_ref[:, p, :] = weights / total - chosen
        loss_ref[:, p : p + 1] = jnp.log(total) + highest - picked

    prior_copy().wait_send()
    for k in range(1, NY):
        query_copy(k).wait_send()
        back_copy(k).wait_send()
    for half in range(2):
        for a, b in plane:
            doc_copy(half, a, b).wait_send()


def on_device(queries, query_lens, documents, doc_lens, positives):
    vmem = pl.BlockSpec(memory_space=pltpu.VMEM)
    smem = pl.BlockSpec(memory_space=pltpu.SMEM)
    dma = pltpu.SemaphoreType.DMA
    return pl.pallas_call(
        kernel,
        out_shape=(
            jax.ShapeDtypeStruct((8, 3, 128), F32),
            jax.ShapeDtypeStruct((8, 3), F32),
        ),
        in_specs=[vmem, vmem, smem, smem, smem],
        out_specs=(vmem, vmem),
        scratch_shapes=[
            pltpu.VMEM((8, 256, 128), BF16),
            pltpu.VMEM((8, 3, 256, 128), BF16),
            pltpu.VMEM((2, 2, 4, 256, 128), BF16),
            pltpu.VMEM((3, 2, 2, 4, 256, 128), F32),
            pltpu.VMEM((8, 3, 2, 2, 4, 8, 256), F32),
            pltpu.VMEM((8, 16, 128), F32),
            pltpu.VMEM((8, 16, 128), F32),
            pltpu.VMEM((16, 8, 128), F32),
            dma((8,)), dma((8,)), dma((16,)), dma((16,)), dma((1,)), dma((1,)), dma((8,)), dma((8,)),
        ],
        compiler_params=pltpu.CompilerParams(
            collective_id=0, has_side_effects=True, vmem_limit_bytes=48 * 2**20
        ),
        name="late_interaction",
    )(queries.reshape(256, 128), documents.reshape(256, 128), query_lens, doc_lens, positives)


def solution(mesh):
    both = ("blk", "grp")
    return jax.shard_map(
        on_device,
        mesh=mesh,
        in_specs=(P(both, None, None), P(both), P(both, None, None), P(both), P(both)),
        out_specs=(P(both, None, None), P(both, None)),
        check_vma=False,
    )
```

time: 721 us -> 52.1 us (0.07)
  the two profiles are of different devices: /device:TPU:8 before, /device:TPU:64 now
where the time goes in v1:
time: 52.1 us; the launch traced here: 51.9 us
  Pallas kernels  47 us (90%)
  local copies, waits for them, and re-layouts  3.59 us (7%)
  between operations  1.3 us (2%)
    pallas_call x1, Pallas kernels, on_device(): pl.pallas_call(kernel, out_shape=(jax.ShapeDtypeStruct((8, 3, 128), F32),...  47 us
    unnamed x8, local copies, waits for them, and re-layouts  2.33 us
    pallas_call x2, local copies, waits for them, and re-layouts, on_device(): pl.pallas_call(kernel, out_shape=(jax.ShapeDtypeStruct((8, 3, 128), F32),...  1.25 us

profile of v1, /device:TPU:64, one launch (start us, length us, event | category | flops | bytes accessed | tf_op | source)
XLA Modules:
  0.0 51.9 jit_solution(8794259474567232695)
XLA Ops:
  1.3 0.0 copy-start.2
  1.3 0.0 copy-start.3
  1.3 0.6 %copy-done.2 = s32[8]{0:T(128)S(1)} copy-done((s32[8]{0:T(128)S(1)}, s32[8]{0:T(128)}, u32[]{:S(2)}) %copy-start.2) | copy-done | bytes 56
  1.9 0.0 copy-done.3
  1.9 0.0 copy-start
  2.0 0.8 %copy-done = bf16[8,32,128]{2,1,0:T(8,128)(2,1)S(1)} copy-done((bf16[8,32,128]{2,1,0:T(8,128)(2,1)S(1)}, bf16[8,32,128]{2,1,0:T(8,128)(2,1)}, u32[]{:S(2)}) %copy-start) | copy-done | bytes 65560
  2.8 0.0 copy-start.1
  2.8 0.8 %copy-done.1 = bf16[1,256,128]{2,1,0:T(8,128)(2,1)S(1)} copy-done((bf16[1,256,128]{2,1,0:T(8,128)(2,1)S(1)}, bf16[1,256,128]{2,1,0:T(8,128)(2,1)}, u32[]{:S(2)}) %copy-start.1) | copy-done | bytes 65560
  3.6 47.0 %late_interaction.1 = (f32[8,3,128]{2,1,0:T(4,128)S(1)}, f32[8,3]{1,0:T(8,128)S(1)}) custom-call(bf16[256,128]{1,0:T(8,128)(2,1)S(1)} %bitcast.2, bf16[256,128]{1,0:T(8,128)(2,1)S(1)} %bitcast.3, s32[8]{0:T(128)S(1)} %copy-done.2, s32[1]{0:T(128)S(6)} %copy.9.dlen_ref, s32[8]{0:T(128)S(1)} %copy-done.3), custom_call_target="tpu_custom_call" | custom-call | tf_op jit(solution)/shard_map/late_interaction/pallas_call | solution.py:241
  50.7 0.6 %copy.7 = f32[8,3,128]{2,0,1:T(8,128)} copy(f32[8,3,128]{2,1,0:T(4,128)S(1)} %get-tuple-element.2) | data formatting | bytes 24576 | tf_op jit(solution)/shard_map/late_interaction/pallas_call | solution.py:241
  51.3 0.7 %copy.8 = f32[8,3]{0,1:T(4,128)} copy(f32[8,3]{1,0:T(8,128)S(1)} %get-tuple-element.3) | data formatting | bytes 192 | tf_op jit(solution)/shard_map/late_interaction/pallas_call | solution.py:241
Async XLA Ops:
  1.3 0.7 %copy-start.2 = (s32[8]{0:T(128)S(1)}, s32[8]{0:T(128)}, u32[]{:S(2)}) copy-start(s32[8]{0:T(128)} %qlen_ref.1) | copy-start | bytes 100
  1.3 0.7 %copy-start.3 = (s32[8]{0:T(128)S(1)}, s32[8]{0:T(128)}, u32[]{:S(2)}) copy-start(s32[8]{0:T(128)} %pos_ref.1) | copy-start | bytes 100
  1.9 0.8 %copy-start = (bf16[8,32,128]{2,1,0:T(8,128)(2,1)S(1)}, bf16[8,32,128]{2,1,0:T(8,128)(2,1)}, u32[]{:S(2)}) copy-start(bf16[8,32,128]{2,1,0:T(8,128)(2,1)} %param.5) | copy-start | bytes 196612
  2.8 0.8 %copy-start.1 = (bf16[1,256,128]{2,1,0:T(8,128)(2,1)S(1)}, bf16[1,256,128]{2,1,0:T(8,128)(2,1)}, u32[]{:S(2)}) copy-start(bf16[1,256,128]{2,1,0:T(8,128)(2,1)} %param.7) | copy-start | bytes 196612

commit v2 on v1

v2 whole, which is shorter than its diff:
```python
import jax
import jax.numpy as jnp
from jax import lax
from jax.experimental import pallas as pl
from jax.experimental.pallas import tpu as pltpu
from jax.sharding import PartitionSpec as P

MESH = pl.DeviceIdType.MESH
F32 = jnp.float32
BF16 = jnp.bfloat16
EPS = 1e-06
FAR = 1e30
HEAT = 20.0
PREFIXES = (64, 96, 128)
NX, NY, NZ = 4, 8, 2
LAST = (((1,), (1,)), ((), ()))


def offset(k):
    return ((k + 1) // 2) * (2 * (k % 2) - 1)


def unit(s):
    i = (s - 4) // 2
    kind = jnp.where(s < 4, jnp.where(s == 1, 1, 0), jnp.where(s < 14, (i + 1) % 2, s - 14))
    k = jnp.where(s < 4, jnp.maximum(s - 1, 0), jnp.where(s < 14, 1 + 2 * ((i + 1) // 2) + s % 2, 7))
    return kind, k


def kernel(
    q_ref, d_ref, qlen_ref, dlen_ref, pos_ref, grad_ref, loss_ref,
    q_own, d_own, q_mine, d_mine, qs, ws, ds, rd, rq, peaks, piece, parts, frame, in_sem,
    x_sem, z_send, z_recv, ring_send, ring_recv, sib_send, sib_recv, d_send, d_recv, r_send, r_recv,
):
    blk, grp = lax.axis_index("blk"), lax.axis_index("grp")
    zl, x, y = blk // (NX * NY), (blk // NY) % NX, blk % NY
    slab, core = grp // 2, grp % 2
    slabs = lax.axis_size("grp") // 2
    direct = zl == core
    kind = jnp.where(direct, 0, 1)
    half = 1 - kind
    older = jnp.logical_and(zl == 0, core == 1)
    fetch = jnp.logical_and(older, slab > 0)
    keeps = jnp.logical_not(fetch)
    hands_on = jnp.logical_and(core == 1, slab < slabs - 1)
    to_partner = jnp.logical_not(jnp.logical_and(zl == 1, core == 1))
    from_partner = jnp.logical_not(older)
    first = jnp.maximum(zl, core)

    def at(z_, x_, y_, slab_, core_):
        return ((z_ * NX + x_) * NY + y_, slab_ * 2 + core_)

    def along_y(by):
        return at(zl, x, (y + by + NY) % NY, slab, core)

    def along_x(by):
        return at(zl, (x + by + NX) % NX, y, slab, core)

    sibling = at(zl, x, y, slab, 1 - core)
    partner = at(1 - zl, x, y, slab, core)
    crossed = at(1 - zl, x, y, slab, 1 - core)
    ahead = at(0, x, y, slab + 1, 1)

    def remote(src, dst, send, recv, to):
        return pltpu.make_async_remote_copy(
            src_ref=src, dst_ref=dst, send_sem=send, recv_sem=recv, device_id=to, device_id_type=MESH
        )

    loads = [
        pltpu.make_async_copy(q_ref, q_own, in_sem.at[0]),
        pltpu.make_async_copy(d_ref, d_own, in_sem.at[1]),
    ]
    for load in loads:
        load.start()

    barrier = pltpu.get_barrier_semaphore()

    def greet(other):
        pl.semaphore_signal(barrier, inc=1, device_id=other, device_id_type=MESH)

    for other in (along_y(1), along_y(-1), sibling, along_x(1), along_x(-1), along_x(2)):
        greet(other)
    pl.when(from_partner)(lambda: greet(partner))
    pl.when(kind == 1)(lambda: greet(crossed))

    @pl.when(fetch)
    def _():
        greet(at(0, x, y, slab - 1, 1))
        greet(at(1, x, y, slab - 1, 1))

    expected = 6 + to_partner.astype(jnp.int32) + kind + hands_on.astype(jnp.int32)

    for load in loads:
        load.wait()

    tokens = lax.broadcasted_iota(jnp.int32, (32, 128), 0)
    for i in range(8):
        rows = q_own[pl.ds(32 * i, 32), :].astype(F32)
        q_mine[pl.ds(32 * i, 32), :] = jnp.where(tokens < qlen_ref[i], rows, 0.0).astype(BF16)
    doc = d_own[...].astype(F32)
    slots = lax.broadcasted_iota(jnp.int32, (256, 128), 0)
    d_mine[...] = jnp.where(slots < dlen_ref[0], doc, doc[0:1, :]).astype(BF16)

    @pl.when(direct)
    def _():
        qs[0, 0] = q_mine[...]

    @pl.when(keeps)
    def _():
        ds[zl, 0] = d_mine[...]

    @pl.when(jnp.logical_and(keeps, older))
    def _():
        ds[1, 0] = d_mine[...]

    pl.semaphore_wait(barrier, expected)

    def cross_copy():
        return remote(q_mine, qs.at[1, 0], x_sem.at[0], x_sem.at[1], crossed)

    def partner_copy():
        return remote(d_mine, ds.at[zl, 0], z_send.at[0], z_recv.at[0], partner)

    def ahead_copy():
        return remote(d_mine, ds.at[zl, 0], z_send.at[1], z_recv.at[1 + zl], ahead)

    def behind_copy(slot):
        return remote(d_mine, ds.at[slot, 0], z_send.at[1], z_recv.at[1 + slot], ahead)

    def ring_copy(k):
        if k == 7:
            rows = pl.ds(0, 128)
            return remote(
                qs.at[kind, 5, rows], qs.at[kind, 7, rows], ring_send.at[7], ring_recv.at[7], along_y(1)
            )
        if k == 8:
            rows = pl.ds(128, 128)
            return remote(
                qs.at[kind, 6, rows], qs.at[kind, 7, rows], ring_send.at[8], ring_recv.at[8], along_y(-1)
            )
        return remote(
            qs.at[kind, max(k - 2, 0)], qs.at[kind, k], ring_send.at[k], ring_recv.at[k],
            along_y(1 if k % 2 else -1),
        )

    def sib_copy(k):
        return remote(qs.at[kind, k], qs.at[kind, k], sib_send.at[k], sib_recv.at[k], sibling)

    def sib_wait(k):
        remote(qs.at[1 - kind, k], qs.at[1 - kind, k], sib_send.at[k], sib_recv.at[k], sibling).wait_recv()

    def doc_copy(slot, b):
        return remote(ds.at[slot, 0], ds.at[slot, b], d_send.at[slot, b], d_recv.at[slot, b], along_x(b))

    def enter():
        ring_copy(1).start()
        ring_copy(2).start()
        sib_copy(0).start()

    def pass_on(arrived, onward):
        for k in arrived:
            ring_copy(k).wait_recv()
        for k in onward:
            ring_copy(k).start()
        for k in arrived:
            if k < 8:
                sib_copy(k).start()

    def spread(slot):
        for b in (1, 3, 2):
            doc_copy(slot, b).start()

    pl.when(kind == 1)(lambda: cross_copy().start())
    pl.when(direct)(enter)
    pl.when(to_partner)(lambda: partner_copy().start())
    pl.when(hands_on)(lambda: ahead_copy().start())

    @pl.when(keeps)
    def _():
        spread(first)

    @pl.when(jnp.logical_and(keeps, older))
    def _():
        spread(1 - first)

    @pl.when(kind == 1)
    def _():
        cross_copy().wait_recv()
        enter()

    @pl.when(fetch)
    def _():
        behind_copy(1).wait_recv()
        spread(1)
        behind_copy(0).wait_recv()
        spread(0)

    @pl.when(from_partner)
    def _():
        remote(d_mine, ds.at[1 - zl, 0], z_send.at[0], z_recv.at[0], partner).wait_recv()
        spread(1 - zl)

    lanes = lax.broadcasted_iota(jnp.int32, (256, 128), 1)
    prefix_rows = lax.broadcasted_iota(jnp.int32, (8, 128), 0)
    prefix_lanes = lax.broadcasted_iota(jnp.int32, (8, 128), 1)
    limit = jnp.where(prefix_rows == 0, 64, jnp.where(prefix_rows == 1, 96, 128))
    below = (prefix_lanes < limit).astype(F32).astype(BF16)
    seg_rows = lax.broadcasted_iota(jnp.int32, (128, 256), 0)
    seg_query = lax.broadcasted_iota(jnp.int32, (128, 256), 1) // 32

    def split(value):
        high = value.astype(BF16)
        return high, value - high.astype(F32)

    def prepare(s):
        kind_, k = unit(s)
        q = qs[kind_, k].astype(F32)
        for p in range(2):
            ws[s, p] = jnp.where(lanes < PREFIXES[p], q, 0.0).astype(BF16)
        ws[s, 2] = qs[kind_, k]
        high, rest = split(q * q)
        sums = lax.dot_general(below, high, LAST, preferred_element_type=F32)
        sums += lax.dot_general(below, rest.astype(BF16), LAST, preferred_element_type=F32)
        rq[s] = lax.rsqrt(sums + EPS) * HEAT

    wide_rows = lax.broadcasted_iota(jnp.int32, (256, 128), 0)
    ones = (lanes < jnp.where(wide_rows < 128, 64, 96)).astype(F32).astype(BF16)

    def norms(slot):
        values = ds[slot].reshape(1024, 128).astype(F32)
        squares = values * values
        high, rest = split(squares)
        sums = lax.dot_general(high, ones, LAST, preferred_element_type=F32)
        sums += lax.dot_general(rest.astype(BF16), ones, LAST, preferred_element_type=F32)
        for p in range(2):
            rd[p, slot] = lax.rsqrt(sums[:, 128 * p : 128 * p + 128] + EPS)
        total = jnp.sum(squares, axis=1, keepdims=True)
        rd[2, slot] = jnp.broadcast_to(lax.rsqrt(total + EPS), (1024, 128))

    def job(s, slot):
        docs = ds[slot].reshape(1024, 128)
        for p in range(3):
            dots = lax.dot_general(docs, ws[s, p], LAST, preferred_element_type=F32)
            scale = rd[p, slot]
            for c in range(2):
                scaled = dots[:, c * 128 : (c + 1) * 128] * scale
                best = jnp.max(jnp.max(scaled.reshape(4, 32, 8, 128), axis=1), axis=1)
                peaks[s, p, slot, :, pl.ds(c * 128, 128)] = best

    def finish(s):
        total = jnp.zeros((8, 128), F32)
        for p in range(3):
            best = peaks[s, p].reshape(8, 256) * rq[s, p : p + 1, :]
            seg = (seg_rows == seg_query + 8 * p).astype(F32).astype(BF16)
            high, rest = split(best)
            middle, rest = split(rest)
            for part in (high, middle, rest.astype(BF16)):
                total += lax.dot_general(part, seg, LAST, preferred_element_type=F32)
        piece[s] = total

    def back_copy(s):
        kind_, k = unit(s)
        home = at(jnp.where(kind_ == 0, zl, 1 - zl), x, (y - offset(k) + NY) % NY, slab, zl)
        return remote(piece.at[s], parts.at[half, y], r_send.at[s], r_recv.at[half, k], home)

    def is_home(s):
        return jnp.logical_and(direct, s == 0)

    def send_back(s):
        pl.when(jnp.logical_not(is_home(s)))(lambda: back_copy(s).start())

        @pl.when(is_home(s))
        def _():
            parts[half, y] = piece[s]

    @pl.when(direct)
    def _():
        pass_on((1, 2), (3, 4))
        sib_wait(0)

    @pl.when(kind == 1)
    def _():
        for k in range(3):
            sib_wait(k)

    for s in range(4):
        prepare(jnp.int32(s))

    def early(j, carry):
        slot = jnp.where(j == 0, first, 1 - first)
        for b in range(1, NX):
            doc_copy(slot, b).wait_recv()
        norms(slot)
        for s in range(4):
            job(s, slot)

        @pl.when(j == 0)
        def _():
            pl.when(kind == 1)(lambda: pass_on((1, 2), (3, 4)))
            pl.when(direct)(lambda: pass_on((3, 4), (5, 6)))

        return carry

    lax.fori_loop(0, 2, early, 0)

    def later(i, carry):
        s = 4 + 2 * i
        kind_, k = unit(s)

        @pl.when(i == 1)
        def _():
            pl.when(direct)(lambda: pass_on((5, 6), (7, 8)))
            pl.when(kind == 1)(lambda: pass_on((3, 4), (5, 6)))

        @pl.when(i == 3)
        def _():
            pl.when(direct)(lambda: pass_on((8, 7), ()))
            pl.when(kind == 1)(lambda: pass_on((5, 6), (7, 8)))

        @pl.when(kind_ != kind)
        def _():
            sib_wait(k)
            sib_wait(k + 1)

        finish(2 * i)
        finish(2 * i + 1)
        for j in range(2):
            prepare(s + j)
            for slot in range(2):
                job(s + j, slot)
        send_back(2 * i)
        send_back(2 * i + 1)
        return carry

    lax.fori_loop(0, 5, later, 0)

    pl.when(kind == 1)(lambda: pass_on((8, 7), ()))

    def last(i, carry):
        s = 14 + i
        kind_, k = unit(s)
        pl.when(kind_ != kind)(lambda: sib_wait(k))
        finish(10 + 2 * i)
        finish(11 + 2 * i)
        prepare(s)
        for slot in range(2):
            job(s, slot)
        send_back(10 + 2 * i)
        send_back(11 + 2 * i)
        return carry

    lax.fori_loop(0, 2, last, 0)
    finish(14)
    finish(15)
    send_back(jnp.int32(14))
    send_back(jnp.int32(15))

    for h in range(2):
        for k in range(NY):
            back = remote(piece.at[0], parts.at[h, (y + offset(k) + NY) % NY], r_send.at[0], r_recv.at[h, k], sibling)
            if h == 1 and k == 0:
                pl.when(kind == 1)(lambda: back.wait_recv())
            else:
                back.wait_recv()

    for h in range(2):
        for slot in range(NZ):
            for b in range(NX):
                column = h * 8 + slot * 4 + (x - b + NX) % NX
                frame[column] = parts[h, :, slot * 4 + b, :]
    logits = jnp.transpose(frame[...].reshape(128, 128))
    columns = lax.broadcasted_iota(jnp.int32, (8, 128), 1)
    rows = lax.broadcasted_iota(jnp.int32, (8, 128), 0)
    valid = jnp.logical_or(columns >= 64, grp > 0)
    target = jnp.zeros((8, 128), jnp.int32)
    for i in range(8):
        target = jnp.where(rows == i, pos_ref[i] + 64, target)
    chosen = (columns == target).astype(F32)
    for p in range(3):
        value = logits[8 * p : 8 * p + 8, :]
        held = jnp.where(valid, value, -FAR)
        highest = jnp.max(held, axis=1, keepdims=True)
        weights = jnp.where(valid, jnp.exp(held - highest), 0.0)
        total = jnp.sum(weights, axis=1, keepdims=True)
        picked = jnp.sum(jnp.where(columns == target, value, 0.0), axis=1, keepdims=True)
        grad_ref[p] = weights / total - chosen
        losses = jnp.where(columns == rows, jnp.log(total) + highest - picked, 0.0)
        loss_ref[p : p + 1, :] = jnp.sum(losses, axis=0, keepdims=True)[:, :8]

    pl.when(kind == 1)(lambda: cross_copy().wait_send())
    pl.when(to_partner)(lambda: partner_copy().wait_send())
    pl.when(hands_on)(lambda: ahead_copy().wait_send())
    for k in range(1, 9):
        ring_copy(k).wait_send()
    for k in range(NY):
        sib_copy(k).wait_send()
    for slot in range(2):
        for b in range(1, NX):
            doc_copy(slot, b).wait_send()

    def sent(s, carry):
        pl.when(jnp.logical_not(is_home(s)))(lambda: back_copy(s).wait_send())
        return carry

    lax.fori_loop(0, 16, sent, 0)


def on_device(queries, query_lens, documents, doc_lens, positives):
    vmem = pl.BlockSpec(memory_space=pltpu.VMEM)
    hbm = pl.BlockSpec(memory_space=pl.ANY)
    smem = pl.BlockSpec(memory_space=pltpu.SMEM)
    dma = pltpu.SemaphoreType.DMA
    grad, loss = pl.pallas_call(
        kernel,
        out_shape=(
            jax.ShapeDtypeStruct((3, 8, 128), F32),
            jax.ShapeDtypeStruct((3, 8), F32),
        ),
        in_specs=[hbm, hbm, smem, smem, smem],
        out_specs=(vmem, vmem),
        scratch_shapes=[
            pltpu.VMEM((256, 128), BF16),
            pltpu.VMEM((256, 128), BF16),
            pltpu.VMEM((256, 128), BF16),
            pltpu.VMEM((256, 128), BF16),
            pltpu.VMEM((2, 8, 256, 128), BF16),
            pltpu.VMEM((16, 3, 256, 128), BF16),
            pltpu.VMEM((2, 4, 256, 128), BF16),
            pltpu.VMEM((3, 2, 1024, 128), F32),
            pltpu.VMEM((16, 8, 256), F32),
            pltpu.VMEM((16, 3, 2, 4, 256), F32),
            pltpu.VMEM((16, 8, 128), F32),
            pltpu.VMEM((2, 8, 8, 128), F32),
            pltpu.VMEM((16, 8, 128), F32),
            dma((2,)), dma((2,)), dma((2,)), dma((3,)), dma((9,)), dma((9,)), dma((8,)), dma((8,)),
            dma((2, 4)), dma((2, 4)), dma((16,)), dma((2, 8)),
        ],
        compiler_params=pltpu.CompilerParams(
            collective_id=0, has_side_effects=True, vmem_limit_bytes=60 * 2**20
        ),
        name="late_interaction",
    )(queries.reshape(256, 128), documents.reshape(256, 128), query_lens, doc_lens, positives)
    return jnp.transpose(grad, (1, 0, 2)), jnp.transpose(loss)


def solution(mesh):
    both = ("blk", "grp")
    return jax.shard_map(
        on_device,
        mesh=mesh,
        in_specs=(P(both, None, None), P(both), P(both, None, None), P(both), P(both)),
        out_specs=(P(both, None, None), P(both, None)),
        check_vma=False,
    )
```

time: 52.1 us -> 46.7 us (0.90)
  the two profiles are of different devices: /device:TPU:64 before, /device:TPU:129 now
where the time goes in v2:
time: 46.7 us; the launch traced here: 46.5 us
  Pallas kernels  43.3 us (93%)
  local copies, waits for them, and re-layouts  1.89 us (4%)
  between operations  1.29 us (3%)
    pallas_call x1, Pallas kernels, on_device(): pl.pallas_call(kernel, out_shape=(jax.ShapeDtypeStruct((3, 8, 128), F32),...  43.3 us
    unnamed x4, local copies, waits for them, and re-layouts  1.89 us

profile of v2, /device:TPU:129, one launch (start us, length us, event | category | flops | bytes accessed | tf_op | source)
XLA Modules:
  0.0 46.5 jit_solution(8412028369235087499)
XLA Ops:
  1.3 43.3 %late_interaction.1 = (f32[3,8,128]{2,1,0:T(8,128)}, f32[3,8]{1,0:T(4,128)}) custom-call(bf16[256,128]{1,0:T(8,128)(2,1)} %bitcast.4, bf16[256,128]{1,0:T(8,128)(2,1)} %bitcast.5, s32[8]{0:T(128)} %qlen_ref.1, s32[1]{0:T(128)S(6)} %copy.9.dlen_ref, s32[8]{0:T(128)} %pos_ref.1), custom_call_target="tpu_custom_call" | custom-call | tf_op jit(solution)/shard_map/late_interaction/pallas_call | solution.py:413
  44.6 0.0 copy-start
  44.6 1.3 %copy.10 = f32[8,3,128]{2,0,1:T(8,128)} copy(f32[8,3,128]{2,0,1:T(8,128)} %bitcast.6) | data formatting | bytes 24576
  45.9 0.0 copy-done
  45.9 0.6 %copy.11 = f32[8,3]{0,1:T(4,128)} copy(f32[8,3]{0,1:T(4,128)S(1)} %bitcast.7) | data formatting | bytes 192
Async XLA Ops:
  44.6 1.3 %copy-start = (f32[3,8]{1,0:T(4,128)S(1)}, f32[3,8]{1,0:T(4,128)}, u32[]{:S(2)}) copy-start(f32[3,8]{1,0:T(4,128)} %get-tuple-element.5) | copy-start | bytes 292

commit v3 on v2

--- a/solution.py
+++ b/solution.py
@@ -21,16 +21,16 @@
 
 
 def unit(s):
-    i = (s - 4) // 2
-    kind = jnp.where(s < 4, jnp.where(s == 1, 1, 0), jnp.where(s < 14, (i + 1) % 2, s - 14))
-    k = jnp.where(s < 4, jnp.maximum(s - 1, 0), jnp.where(s < 14, 1 + 2 * ((i + 1) // 2) + s % 2, 7))
+    kind = jnp.where(s < 6, jnp.where((s == 1) | (s > 3), 1, 0), jnp.where(s < 14, ((s - 6) // 2) % 2, s - 14))
+    near = jnp.where(s < 2, 0, 1 + s % 2)
+    k = jnp.where(s < 6, near, jnp.where(s < 14, 3 + 2 * ((s - 6) // 4) + s % 2, 7))
     return kind, k
 
 
 def kernel(
     q_ref, d_ref, qlen_ref, dlen_ref, pos_ref, grad_ref, loss_ref,
     q_own, d_own, q_mine, d_mine, qs, ws, ds, rd, rq, peaks, piece, parts, frame, in_sem,
-    x_sem, z_send, z_recv, ring_send, ring_recv, sib_send, sib_recv, d_send, d_recv, r_send, r_recv,
+    z_send, z_recv, q_send, q_recv, sib_send, sib_recv, d_send, d_recv, r_send, r_recv,
 ):
     blk, grp = lax.axis_index("blk"), lax.axis_index("grp")
     zl, x, y = blk // (NX * NY), (blk // NY) % NX, blk % NY
@@ -58,7 +58,10 @@
 
     sibling = at(zl, x, y, slab, 1 - core)
     partner = at(1 - zl, x, y, slab, core)
-    crossed = at(1 - zl, x, y, slab, 1 - core)
+
+    def crossed(by):
+        return at(1 - zl, x, (y + by + NY) % NY, slab, 1 - core)
+
     ahead = at(0, x, y, slab + 1, 1)
 
     def remote(src, dst, send, recv, to):
@@ -78,17 +81,24 @@
     def greet(other):
         pl.semaphore_signal(barrier, inc=1, device_id=other, device_id_type=MESH)
 
-    for other in (along_y(1), along_y(-1), sibling, along_x(1), along_x(-1), along_x(2)):
+    for other in (sibling, along_x(1), along_x(-1), along_x(2)):
         greet(other)
     pl.when(from_partner)(lambda: greet(partner))
-    pl.when(kind == 1)(lambda: greet(crossed))
+
+    for by in (1, -1, 2, -2):
+        greet(along_y(by))
+
+    @pl.when(kind == 1)
+    def _():
+        for by in (0, 1, -1, 2, -2):
+            greet(crossed(by))
 
     @pl.when(fetch)
     def _():
         greet(at(0, x, y, slab - 1, 1))
         greet(at(1, x, y, slab - 1, 1))
 
-    expected = 6 + to_partner.astype(jnp.int32) + kind + hands_on.astype(jnp.int32)
+    expected = 8 + to_partner.astype(jnp.int32) + 5 * kind + hands_on.astype(jnp.int32)
 
     for load in loads:
         load.wait()
@@ -115,9 +125,6 @@
 
     pl.semaphore_wait(barrier, expected)
 
-    def cross_copy():
-        return remote(q_mine, qs.at[1, 0], x_sem.at[0], x_sem.at[1], crossed)
-
     def partner_copy():
         return remote(d_mine, ds.at[zl, 0], z_send.at[0], z_recv.at[0], partner)
 
@@ -127,21 +134,21 @@
     def behind_copy(slot):
         return remote(d_mine, ds.at[slot, 0], z_send.at[1], z_recv.at[1 + slot], ahead)
 
+    def query_copy(k):
+        return remote(q_mine, qs.at[0, k], q_send.at[k], q_recv.at[k], along_y(offset(k)))
+
+    def cross_copy(k):
+        return remote(q_mine, qs.at[1, k], q_send.at[k], q_recv.at[k], crossed(offset(k)))
+
     def ring_copy(k):
+        low, high = pl.ds(0, 128), pl.ds(128, 128)
         if k == 7:
-            rows = pl.ds(0, 128)
-            return remote(
-                qs.at[kind, 5, rows], qs.at[kind, 7, rows], ring_send.at[7], ring_recv.at[7], along_y(1)
-            )
-        if k == 8:
-            rows = pl.ds(128, 128)
-            return remote(
-                qs.at[kind, 6, rows], qs.at[kind, 7, rows], ring_send.at[8], ring_recv.at[8], along_y(-1)
-            )
-        return remote(
-            qs.at[kind, max(k - 2, 0)], qs.at[kind, k], ring_send.at[k], ring_recv.at[k],
-            along_y(1 if k % 2 else -1),
-        )
+            src, dst, by = qs.at[kind, 3, low], qs.at[kind, 7, low], 2
+        elif k == 8:
+            src, dst, by = qs.at[kind, 4, high], qs.at[kind, 7, high], -2
+        else:
+            src, dst, by = qs.at[kind, k - 2], qs.at[kind, k], 1 if k == 5 else -1
+        return remote(src, dst, q_send.at[k], q_recv.at[k], along_y(by))
 
     def sib_copy(k):
         return remote(qs.at[kind, k], qs.at[kind, k], sib_send.at[k], sib_recv.at[k], sibling)
@@ -152,29 +159,37 @@
     def doc_copy(slot, b):
         return remote(ds.at[slot, 0], ds.at[slot, b], d_send.at[slot, b], d_recv.at[slot, b], along_x(b))
 
-    def enter():
-        ring_copy(1).start()
-        ring_copy(2).start()
-        sib_copy(0).start()
-
-    def pass_on(arrived, onward):
-        for k in arrived:
-            ring_copy(k).wait_recv()
-        for k in onward:
-            ring_copy(k).start()
-        for k in arrived:
+    def arrived(*ks):
+        for k in ks:
+            (ring_copy if k > 4 else query_copy)(k).wait_recv()
+        if 3 in ks:
+            for k in (5, 6, 7, 8):
+                ring_copy(k).start()
+        for k in ks:
             if k < 8:
                 sib_copy(k).start()
+
+    def shared(*ks):
+        for k in ks:
+            sib_wait(k)
 
     def spread(slot):
         for b in (1, 3, 2):
             doc_copy(slot, b).start()
 
-    pl.when(kind == 1)(lambda: cross_copy().start())
-    pl.when(direct)(enter)
     pl.when(to_partner)(lambda: partner_copy().start())
     pl.when(hands_on)(lambda: ahead_copy().start())
 
+    @pl.when(direct)
+    def _():
+        for k in (1, 2):
+            query_copy(k).start()
+
+    @pl.when(kind == 1)
+    def _():
+        for k in range(3):
+            cross_copy(k).start()
+
     @pl.when(keeps)
     def _():
         spread(first)
@@ -183,10 +198,16 @@
     def _():
         spread(1 - first)
 
+    @pl.when(direct)
+    def _():
+        sib_copy(0).start()
+        for k in (3, 4):
+            query_copy(k).start()
+
     @pl.when(kind == 1)
     def _():
-        cross_copy().wait_recv()
-        enter()
+        for k in (3, 4):
+            cross_copy(k).start()
 
     @pl.when(fetch)
     def _():
@@ -247,16 +268,30 @@
                 best = jnp.max(jnp.max(scaled.reshape(4, 32, 8, 128), axis=1), axis=1)
                 peaks[s, p, slot, :, pl.ds(c * 128, 128)] = best
 
+    def whole_job(s):
+        docs = ds[...].reshape(2048, 128)
+        for p in range(3):
+            dots = lax.dot_general(docs, ws[s, p], LAST, preferred_element_type=F32)
+            scale = rd[p].reshape(2048, 128)
+            for c in range(2):
+                scaled = dots[:, c * 128 : (c + 1) * 128] * scale
+                best = jnp.max(jnp.max(scaled.reshape(2, 4, 32, 8, 128), axis=2), axis=2)
+                peaks[s, p, :, :, pl.ds(c * 128, 128)] = best
+
     def finish(s):
-        total = jnp.zeros((8, 128), F32)
+        total = jnp.zeros((16, 128), F32)
         for p in range(3):
-            best = peaks[s, p].reshape(8, 256) * rq[s, p : p + 1, :]
+            best = jnp.concatenate(
+                [peaks[s + j, p].reshape(8, 256) * rq[s + j, p : p + 1, :] for j in range(2)], axis=0
+            )
             seg = (seg_rows == seg_query + 8 * p).astype(F32).astype(BF16)
             high, rest = split(best)
             middle, rest = split(rest)
-            for part in (high, middle, rest.astype(BF16)):
-                total += lax.dot_general(part, seg, LAST, preferred_element_type=F32)
-        piece[s] = total
+            parts_ = jnp.concatenate([high, middle, rest.astype(BF16)], axis=0)
+            sums = lax.dot_general(parts_, seg, LAST, preferred_element_type=F32)
+            total += sums[:16] + sums[16:32] + sums[32:]
+        piece[s] = total[:8]
+        piece[s + 1] = total[8:]
 
     def back_copy(s):
         kind_, k = unit(s)
@@ -275,85 +310,91 @@
 
     @pl.when(direct)
     def _():
-        pass_on((1, 2), (3, 4))
-        sib_wait(0)
+        arrived(1, 2)
+        shared(0)
 
     @pl.when(kind == 1)
     def _():
-        for k in range(3):
-            sib_wait(k)
+        arrived(0)
+        shared(0, 1, 2)
+        arrived(1, 2)
+
+    def wait_docs(slot):
+        for b in range(1, NX):
+            doc_copy(slot, b).wait_recv()
 
     for s in range(4):
         prepare(jnp.int32(s))
-
-    def early(j, carry):
-        slot = jnp.where(j == 0, first, 1 - first)
-        for b in range(1, NX):
-            doc_copy(slot, b).wait_recv()
-        norms(slot)
-        for s in range(4):
-            job(s, slot)
-
-        @pl.when(j == 0)
+    wait_docs(first)
+    norms(first)
+    for s in range(4):
+        job(s, first)
+    pl.when(direct)(lambda: shared(1, 2))
+    for s in range(4, 6):
+        prepare(jnp.int32(s))
+        job(s, first)
+    wait_docs(1 - first)
+    pl.when(direct)(lambda: arrived(3, 4))
+    norms(1 - first)
+    for s in range(2, 4):
+        job(s, 1 - first)
+
+    def later(i, carry):
+        s = 6 + 2 * i
+        done = jnp.where(i == 0, 2, 4 + 2 * i)
+
+        @pl.when(kind == 1)
         def _():
-            pl.when(kind == 1)(lambda: pass_on((1, 2), (3, 4)))
-            pl.when(direct)(lambda: pass_on((3, 4), (5, 6)))
-
-        return carry
-
-    lax.fori_loop(0, 2, early, 0)
-
-    def later(i, carry):
-        s = 4 + 2 * i
-        kind_, k = unit(s)
-
-        @pl.when(i == 1)
+            @pl.when(i == 0)
+            def _():
+                shared(3, 4)
+                arrived(3, 4)
+
+            @pl.when(i == 2)
+            def _():
+                shared(5, 6)
+                arrived(5, 6)
+
+            pl.when(i == 3)(lambda: arrived(8, 7))
+            pl.when(i == 4)(lambda: shared(7))
+
+        @pl.when(direct)
         def _():
-            pl.when(direct)(lambda: pass_on((5, 6), (7, 8)))
-            pl.when(kind == 1)(lambda: pass_on((3, 4), (5, 6)))
-
-        @pl.when(i == 3)
-        def _():
-            pl.when(direct)(lambda: pass_on((8, 7), ()))
-            pl.when(kind == 1)(lambda: pass_on((5, 6), (7, 8)))
-
-        @pl.when(kind_ != kind)
-        def _():
-            sib_wait(k)
-            sib_wait(k + 1)
-
-        finish(2 * i)
-        finish(2 * i + 1)
+            @pl.when(i == 1)
+            def _():
+                shared(3, 4)
+                arrived(5, 6)
+
+            @pl.when(i == 3)
+            def _():
+                shared(5, 6)
+                arrived(8, 7)
+
+            pl.when(i == 4)(lambda: shared(7))
+
+        finish(done)
         for j in range(2):
             prepare(s + j)
-            for slot in range(2):
-                job(s + j, slot)
-        send_back(2 * i)
-        send_back(2 * i + 1)
+            whole_job(s + j)
+        send_back(done)
+        send_back(done + 1)
         return carry
 
     lax.fori_loop(0, 5, later, 0)
 
-    pl.when(kind == 1)(lambda: pass_on((8, 7), ()))
-
-    def last(i, carry):
-        s = 14 + i
-        kind_, k = unit(s)
-        pl.when(kind_ != kind)(lambda: sib_wait(k))
-        finish(10 + 2 * i)
-        finish(11 + 2 * i)
-        prepare(s)
-        for slot in range(2):
-            job(s, slot)
-        send_back(10 + 2 * i)
-        send_back(11 + 2 * i)
-        return carry
-
-    lax.fori_loop(0, 2, last, 0)
     finish(14)
-    finish(15)
     send_back(jnp.int32(14))
     send_back(jnp.int32(15))
+    for s in (4, 5):
+        job(s, 1 - first)
+    finish(4)
+    for s in (4, 5):
+        send_back(jnp.int32(s))
+    for s in (0, 1):
+        job(s, 1 - first)
+    finish(0)
+    for s in (0, 1):
+        send_back(jnp.int32(s))
 
     for h in range(2):
         for k in range(NY):
@@ -383,14 +424,15 @@
         weights = jnp.where(valid, jnp.exp(held - highest), 0.0)
         total = jnp.sum(weights, axis=1, keepdims=True)
         picked = jnp.sum(jnp.where(columns == target, value, 0.0), axis=1, keepdims=True)
-        grad_ref[p] = weights / total - chosen
-        losses = jnp.where(columns == rows, jnp.log(total) + highest - picked, 0.0)
-        loss_ref[p : p + 1, :] = jnp.sum(losses, axis=0, keepdims=True)[:, :8]
-
-    pl.when(kind == 1)(lambda: cross_copy().wait_send())
+        grad_ref[:, p, :] = weights / total - chosen
+        loss_ref[:, p : p + 1] = jnp.log(total) + highest - picked
+
+    pl.when(kind == 1)(lambda: cross_copy(0).wait_send())
     pl.when(to_partner)(lambda: partner_copy().wait_send())
     pl.when(hands_on)(lambda: ahead_copy().wait_send())
-    for k in range(1, 9):
+    for k in range(1, 5):
+        query_copy(k).wait_send()
+    for k in range(5, 9):
         ring_copy(k).wait_send()
     for k in range(NY):
         sib_copy(k).wait_send()
@@ -407,14 +449,18 @@
 
 def on_device(queries, query_lens, documents, doc_lens, positives):
     vmem = pl.BlockSpec(memory_space=pltpu.VMEM)
-    hbm = pl.BlockSpec(memory_space=pl.ANY)
+    hbm = pl.BlockSpec(memory_space=pltpu.HBM)
     smem = pl.BlockSpec(memory_space=pltpu.SMEM)
     dma = pltpu.SemaphoreType.DMA
-    grad, loss = pl.pallas_call(
+    far = [
+        pltpu.with_memory_space_constraint(block.reshape(256, 128), pltpu.HBM)
+        for block in (queries, documents)
+    ]
+    return pl.pallas_call(
         kernel,
         out_shape=(
-            jax.ShapeDtypeStruct((3, 8, 128), F32),
-            jax.ShapeDtypeStruct((3, 8), F32),
+            jax.ShapeDtypeStruct((8, 3, 128), F32),
+            jax.ShapeDtypeStruct((8, 3), F32),
         ),
         in_specs=[hbm, hbm, smem, smem, smem],
         out_specs=(vmem, vmem),
@@ -432,15 +478,14 @@
             pltpu.VMEM((16, 8, 128), F32),
             pltpu.VMEM((2, 8, 8, 128), F32),
             pltpu.VMEM((16, 8, 128), F32),
-            dma((2,)), dma((2,)), dma((2,)), dma((3,)), dma((9,)), dma((9,)), dma((8,)), dma((8,)),
+            dma((2,)), dma((2,)), dma((3,)), dma((9,)), dma((9,)), dma((8,)), dma((8,)),
             dma((2, 4)), dma((2, 4)), dma((16,)), dma((2, 8)),
         ],
         compiler_params=pltpu.CompilerParams(
-            collective_id=0, has_side_effects=True, vmem_limit_bytes=60 * 2**20
+            collective_id=0, has_side_effects=True, vmem_limit_bytes=32 * 2**20
         ),
         name="late_interaction",
-    )(queries.reshape(256, 128), documents.reshape(256, 128), query_lens, doc_lens, positives)
-    return jnp.transpose(grad, (1, 0, 2)), jnp.transpose(loss)
+    )(*far, query_lens, doc_lens, positives)
 
 
 def solution(mesh):

time: 46.7 us -> 42.4 us (0.908)
  Pallas kernels: 43.3 us -> 39 us
    pallas_call x1, Pallas kernels: 43.3 us -> 39 us  [on_device(): pl.pallas_call(kernel, out_shape=(jax.ShapeDtypeStruct((8, 3, 128), F32),...]
    pallas_call x0 -> x2, local copies, waits for them, and re-layouts: none -> 1.25 us  [on_device(): pl.pallas_call(kernel, out_shape=(jax.ShapeDtypeStruct((8, 3, 128), F32),...]
    unnamed x4, local copies, waits for them, and re-layouts: 1.89 us -> 0.66 us
where the time goes in v3:
time: 42.4 us; the launch traced here: 42.2 us
  Pallas kernels  39 us (92%)
  local copies, waits for them, and re-layouts  1.91 us (5%)
  between operations  1.3 us (3%)
    pallas_call x1, Pallas kernels, on_device(): pl.pallas_call(kernel, out_shape=(jax.ShapeDtypeStruct((8, 3, 128), F32),...  39 us
    pallas_call x2, local copies, waits for them, and re-layouts, on_device(): pl.pallas_call(kernel, out_shape=(jax.ShapeDtypeStruct((8, 3, 128), F32),...  1.25 us

profile of v3, /device:TPU:129, one launch (start us, length us, event | category | flops | bytes accessed | tf_op | source)
XLA Modules:
  0.0 42.2 jit_solution(10922157858922815544)
XLA Ops:
  1.3 0.0 copy-start
  1.3 0.0 copy-start.1
  1.3 0.6 %copy-done = s32[8]{0:T(128)S(1)} copy-done((s32[8]{0:T(128)S(1)}, s32[8]{0:T(128)}, u32[]{:S(2)}) %copy-start) | copy-done | bytes 56
  1.9 0.0 copy-done.1
  1.9 39.0 %late_interaction.1 = (f32[8,3,128]{2,1,0:T(4,128)S(1)}, f32[8,3]{1,0:T(8,128)S(1)}) custom-call(bf16[256,128]{1,0:T(8,128)(2,1)} %bitcast.2, bf16[256,128]{1,0:T(8,128)(2,1)} %bitcast.3, s32[8]{0:T(128)S(1)} %copy-done, s32[1]{0:T(128)S(6)} %copy.9.dlen_ref, s32[8]{0:T(128)S(1)} %copy-done.1), custom_call_target="tpu_custom_call" | custom-call | tf_op jit(solution)/shard_map/late_interaction/pallas_call | solution.py:459
  40.9 0.6 %copy.7 = f32[8,3,128]{2,0,1:T(8,128)} copy(f32[8,3,128]{2,1,0:T(4,128)S(1)} %get-tuple-element.2) | data formatting | bytes 24576 | tf_op jit(solution)/shard_map/late_interaction/pallas_call | solution.py:459
  41.5 0.7 %copy.8 = f32[8,3]{0,1:T(4,128)} copy(f32[8,3]{1,0:T(8,128)S(1)} %get-tuple-element.3) | data formatting | bytes 192 | tf_op jit(solution)/shard_map/late_interaction/pallas_call | solution.py:459
Async XLA Ops:
  1.3 0.7 %copy-start = (s32[8]{0:T(128)S(1)}, s32[8]{0:T(128)}, u32[]{:S(2)}) copy-start(s32[8]{0:T(128)} %qlen_ref.1) | copy-start | bytes 100
  1.3 0.7 %copy-start.1 = (s32[8]{0:T(128)S(1)}, s32[8]{0:T(128)}, u32[]{:S(2)}) copy-start(s32[8]{0:T(128)} %pos_ref.1) | copy-start | bytes 100

commit v4 on v3

--- a/solution.py
+++ b/solution.py
@@ -28,8 +28,8 @@
 
 
 def kernel(
-    q_ref, d_ref, qlen_ref, dlen_ref, pos_ref, grad_ref, loss_ref,
-    q_own, d_own, q_mine, d_mine, qs, ws, ds, rd, rq, peaks, piece, parts, frame, in_sem,
+    q_ref, d_ref, qlen_in, dlen_ref, pos_in, grad_ref, loss_ref,
+    qlen_ref, pos_ref, q_own, d_own, q_mine, d_mine, qs, ws, ds, rd, rq, peaks, piece, parts, frame, in_sem,
     z_send, z_recv, q_send, q_recv, sib_send, sib_recv, d_send, d_recv, r_send, r_recv,
 ):
     blk, grp = lax.axis_index("blk"), lax.axis_index("grp")
@@ -72,6 +72,8 @@
     loads = [
         pltpu.make_async_copy(q_ref, q_own, in_sem.at[0]),
         pltpu.make_async_copy(d_ref, d_own, in_sem.at[1]),
+        pltpu.make_async_copy(qlen_in, qlen_ref, in_sem.at[2]),
+        pltpu.make_async_copy(pos_in, pos_ref, in_sem.at[3]),
     ]
     for load in loads:
         load.start()
@@ -452,9 +454,9 @@
     hbm = pl.BlockSpec(memory_space=pltpu.HBM)
     smem = pl.BlockSpec(memory_space=pltpu.SMEM)
     dma = pltpu.SemaphoreType.DMA
-    far = [
-        pltpu.with_memory_space_constraint(block.reshape(256, 128), pltpu.HBM)
-        for block in (queries, documents)
+    q, d, q_lens, places = [
+        pltpu.with_memory_space_constraint(block, pltpu.HBM)
+        for block in (queries.reshape(256, 128), documents.reshape(256, 128), query_lens, positives)
     ]
     return pl.pallas_call(
         kernel,
@@ -462,9 +464,11 @@
             jax.ShapeDtypeStruct((8, 3, 128), F32),
             jax.ShapeDtypeStruct((8, 3), F32),
         ),
-        in_specs=[hbm, hbm, smem, smem, smem],
+        in_specs=[hbm, hbm, hbm, smem, hbm],
         out_specs=(vmem, vmem),
         scratch_shapes=[
+            pltpu.SMEM((8,), jnp.int32),
+            pltpu.SMEM((8,), jnp.int32),
             pltpu.VMEM((256, 128), BF16),
             pltpu.VMEM((256, 128), BF16),
             pltpu.VMEM((256, 128), BF16),
@@ -478,14 +482,14 @@
             pltpu.VMEM((16, 8, 128), F32),
             pltpu.VMEM((2, 8, 8, 128), F32),
             pltpu.VMEM((16, 8, 128), F32),
-            dma((2,)), dma((2,)), dma((3,)), dma((9,)), dma((9,)), dma((8,)), dma((8,)),
+            dma((4,)), dma((2,)), dma((3,)), dma((9,)), dma((9,)), dma((8,)), dma((8,)),
             dma((2, 4)), dma((2, 4)), dma((16,)), dma((2, 8)),
         ],
         compiler_params=pltpu.CompilerParams(
             collective_id=0, has_side_effects=True, vmem_limit_bytes=32 * 2**20
         ),
         name="late_interaction",
-    )(*far, query_lens, doc_lens, positives)
+    )(q, d, q_lens, doc_lens, places)
 
 
 def solution(mesh):

time: 42.4 us -> 41.2 us (0.972)
  local copies, waits for them, and re-layouts: 1.91 us -> 1.25 us
  Pallas kernels: 39 us -> 38.5 us
    unnamed x4 -> x0, local copies, waits for them, and re-layouts: 0.66 us -> none
    pallas_call x1, Pallas kernels: 39 us -> 38.5 us  [on_device(): pl.pallas_call(kernel, out_shape=(jax.ShapeDtypeStruct((8, 3, 128), F32),...]
where the time goes in v4:
time: 41.2 us; the launch traced here: 41 us
  Pallas kernels  38.5 us (93%)
  between operations  1.29 us (3%)
  local copies, waits for them, and re-layouts  1.25 us (3%)
    pallas_call x1, Pallas kernels, on_device(): pl.pallas_call(kernel, out_shape=(jax.ShapeDtypeStruct((8, 3, 128), F32),...  38.5 us
    pallas_call x2, local copies, waits for them, and re-layouts, on_device(): pl.pallas_call(kernel, out_shape=(jax.ShapeDtypeStruct((8, 3, 128), F32),...  1.25 us

profile of v4, /device:TPU:129, one launch (start us, length us, event | category | flops | bytes accessed | tf_op | source)
XLA Modules:
  0.0 41.0 jit_solution(10914818803334375538)
XLA Ops:
  1.3 38.5 %late_interaction.1 = (f32[8,3,128]{2,1,0:T(4,128)S(1)}, f32[8,3]{1,0:T(8,128)S(1)}) custom-call(bf16[256,128]{1,0:T(8,128)(2,1)} %bitcast.2, bf16[256,128]{1,0:T(8,128)(2,1)} %bitcast.3, s32[8]{0:T(128)} %qlen_in.1, s32[1]{0:T(128)S(6)} %copy.9.dlen_ref, s32[8]{0:T(128)} %pos_in.1), custom_call_target="tpu_custom_call" | custom-call | tf_op jit(solution)/shard_map/late_interaction/pallas_call | solution.py:461
  39.7 0.6 %copy.7 = f32[8,3,128]{2,0,1:T(8,128)} copy(f32[8,3,128]{2,1,0:T(4,128)S(1)} %get-tuple-element.2) | data formatting | bytes 24576 | tf_op jit(solution)/shard_map/late_interaction/pallas_call | solution.py:461
  40.4 0.7 %copy.8 = f32[8,3]{0,1:T(4,128)} copy(f32[8,3]{1,0:T(8,128)S(1)} %get-tuple-element.3) | data formatting | bytes 192 | tf_op jit(solution)/shard_map/late_interaction/pallas_call | solution.py:461

commit v5 on v4

--- a/solution.py
+++ b/solution.py
@@ -105,17 +105,9 @@
     for load in loads:
         load.wait()
 
-    tokens = lax.broadcasted_iota(jnp.int32, (32, 128), 0)
-    for i in range(8):
-        rows = q_own[pl.ds(32 * i, 32), :].astype(F32)
-        q_mine[pl.ds(32 * i, 32), :] = jnp.where(tokens < qlen_ref[i], rows, 0.0).astype(BF16)
     doc = d_own[...].astype(F32)
     slots = lax.broadcasted_iota(jnp.int32, (256, 128), 0)
     d_mine[...] = jnp.where(slots < dlen_ref[0], doc, doc[0:1, :]).astype(BF16)
-
-    @pl.when(direct)
-    def _():
-        qs[0, 0] = q_mine[...]
 
     @pl.when(keeps)
     def _():
@@ -182,6 +174,23 @@
     pl.when(to_partner)(lambda: partner_copy().start())
     pl.when(hands_on)(lambda: ahead_copy().start())
 
+    @pl.when(keeps)
+    def _():
+        spread(first)
+
+    @pl.when(jnp.logical_and(keeps, older))
+    def _():
+        spread(1 - first)
+
+    tokens = lax.broadcasted_iota(jnp.int32, (32, 128), 0)
+    for i in range(8):
+        rows = q_own[pl.ds(32 * i, 32), :].astype(F32)
+        q_mine[pl.ds(32 * i, 32), :] = jnp.where(tokens < qlen_ref[i], rows, 0.0).astype(BF16)
+
+    @pl.when(direct)
+    def _():
+        qs[0, 0] = q_mine[...]
+
     @pl.when(direct)
     def _():
         for k in (1, 2):
@@ -191,14 +200,6 @@
     def _():
         for k in range(3):
             cross_copy(k).start()
-
-    @pl.when(keeps)
-    def _():
-        spread(first)
-
-    @pl.when(jnp.logical_and(keeps, older))
-    def _():
-        spread(1 - first)
 
     @pl.when(direct)
     def _():

time: 41.2 us -> 41.2 us (level)
  no operation moved by 1% of the time
where the time goes in v5:
time: 41.2 us; the launch traced here: 41 us
  Pallas kernels  38.5 us (93%)
  between operations  1.29 us (3%)
  local copies, waits for them, and re-layouts  1.25 us (3%)
    pallas_call x1, Pallas kernels, on_device(): pl.pallas_call(kernel, out_shape=(jax.ShapeDtypeStruct((8, 3, 128), F32),...  38.5 us
    pallas_call x2, local copies, waits for them, and re-layouts, on_device(): pl.pallas_call(kernel, out_shape=(jax.ShapeDtypeStruct((8, 3, 128), F32),...  1.25 us

profile of v5, /device:TPU:129, one launch (start us, length us, event | category | flops | bytes accessed | tf_op | source)
XLA Modules:
  0.0 41.0 jit_solution(17248028958017987264)
XLA Ops:
  1.3 38.5 %late_interaction.1 = (f32[8,3,128]{2,1,0:T(4,128)S(1)}, f32[8,3]{1,0:T(8,128)S(1)}) custom-call(bf16[256,128]{1,0:T(8,128)(2,1)} %bitcast.2, bf16[256,128]{1,0:T(8,128)(2,1)} %bitcast.3, s32[8]{0:T(128)} %qlen_in.1, s32[1]{0:T(128)S(6)} %copy.9.dlen_ref, s32[8]{0:T(128)} %pos_in.1), custom_call_target="tpu_custom_call" | custom-call | tf_op jit(solution)/shard_map/late_interaction/pallas_call | solution.py:462
  39.7 0.6 %copy.7 = f32[8,3,128]{2,0,1:T(8,128)} copy(f32[8,3,128]{2,1,0:T(4,128)S(1)} %get-tuple-element.2) | data formatting | bytes 24576 | tf_op jit(solution)/shard_map/late_interaction/pallas_call | solution.py:462
  40.4 0.7 %copy.8 = f32[8,3]{0,1:T(4,128)} copy(f32[8,3]{1,0:T(8,128)S(1)} %get-tuple-element.3) | data formatting | bytes 192 | tf_op jit(solution)/shard_map/late_interaction/pallas_call | solution.py:462
